TPU v7x, 128 devices: a whole 4x4x4 slice. The times are simulated.
128 devices in a mesh: clus: 4 (over x), split: 32 (over z, y, core).
Axes of the slice: x: 4, y: 4, z: 4, core: 2. Of those that a mesh axis runs over, the one named last changes fastest.
Arguments:
- embeddings: float32 [16384, 4096], P(('clus', 'split'))
- cluster_ids: int32 [16384], P(('clus', 'split')), may hold values from 0 to 63, as said below
Outputs:
- best_similarity: float32 [16384], P(('clus', 'split'))
Inputs may be any that keep to these rules, and one draw needn't show every extreme that they name: `cluster_ids`: the documents of one device's shard hold at most 64 cluster ids with any one residue modulo 4, and every shard has a residue reached exactly 64 times. Some clusters hold a single document.
All inputs are finite; a program needn't handle non-finite values.
Results may differ from a plain program's by a relative error of at most 0.0003.
Values may be sent and summed in bfloat16 or wider, within the bound.
No kernel may reach another device: no remote copies, remote signals or barrier semaphores. Data moves between devices by JAX's collectives and lax.ppermute only.
A program may use at most 192 MiB of HBM per device.

v0:
```python
import jax
import jax.numpy as jnp
from jax import lax
from jax.sharding import PartitionSpec as P


def masked_scores(left, left_ids, right, right_ids, left_start):
    scores = lax.dot_general(
        left, right, (((1,), (1,)), ((), ())), preferred_element_type=jnp.float32
    )
    left_at = left_start + jnp.arange(left.shape[0], dtype=jnp.int32)
    right_at = jnp.arange(right.shape[0], dtype=jnp.int32)
    mask = (
        (left_ids[:, None] == right_ids[None, :])
        & (left_ids[:, None] >= 0)
        & (left_at[:, None] != right_at[None, :])
    )
    return jnp.where(mask, scores, -1.0)


def normalise_rows(values):
    squares = jnp.sum(values * values, axis=1, keepdims=True)
    return (values * lax.rsqrt(squares + 1e-06)).astype(jnp.bfloat16)


def on_device(embeddings, cluster_ids):
    rows = embeddings.shape[0]
    groups = lax.axis_size("clus")
    cap = 2 * rows // groups
    slots = groups * cap
    owner_of = cluster_ids % groups
    onehot = (owner_of[:, None] == jnp.arange(groups, dtype=jnp.int32)[None, :]).astype(jnp.int32)
    before = jnp.cumsum(onehot, axis=0) - onehot
    rank = jnp.sum(before * onehot, axis=1)
    place = owner_of * cap + rank
    picked = place[None, :] == jnp.arange(slots, dtype=jnp.int32)[:, None]
    filled = jnp.any(picked, axis=1)
    source = jnp.sum(jnp.where(picked, jnp.arange(rows, dtype=jnp.int32)[None, :], 0), axis=1)
    out_labels = jnp.where(filled, cluster_ids[source], -1)
    local_unit = normalise_rows(embeddings)
    outgoing_unit = jnp.where(filled[:, None], local_unit[source], jnp.zeros((), jnp.bfloat16))
    unit, labels = (
        lax.all_to_all(outgoing_unit, "clus", split_axis=0, concat_axis=0, tiled=True),
        lax.all_to_all(out_labels, "clus", split_axis=0, concat_axis=0, tiled=True),
    )
    own_start = lax.axis_index("split") * slots
    floor_values = jnp.full((slots,), -1.0, jnp.float32)
    scores = masked_scores(
        unit,
        labels,
        lax.all_gather(unit, "split", axis=0, tiled=True),
        lax.all_gather(labels, "split", axis=0, tiled=True),
        own_start,
    )
    best = jnp.maximum(floor_values, jnp.max(scores, axis=1))
    returned_max = lax.all_to_all(best, "clus", split_axis=0, concat_axis=0, tiled=True)
    return returned_max[place]


def solution(mesh):
    in_specs = (P(("clus", "split"), None), P(("clus", "split")))
    out_specs = P(("clus", "split"))
    return jax.shard_map(
        on_device, mesh=mesh, in_specs=in_specs, out_specs=out_specs, check_vma=False
    )
```

profile of v0, /device:TPU:0, one launch (start us, length us, event | category | flops | bytes accessed | tf_op | source)
XLA Modules:
  0.0 294.9 jit_solution(16780526485380917887)
XLA Ops:
  6.5 0.0 copy-start.1
  6.5 0.0 all-gather.3.cloned.1.call-start
  6.5 0.8 and_select_fusion
  7.4 0.1 fusion.3
  7.4 0.2 reduce_window_sum.11
  7.6 0.2 select_reduce_fusion.1
  7.8 0.7 compare_select_fusion.1
  8.5 0.1 select_reduce_fusion
  8.6 0.1 fusion.2
  8.7 1.8 multiply_reduce_fusion
  10.6 0.0 copy-done.1
  10.6 0.2 multiply_convert_fusion
  10.8 0.1 broadcast_in_dim.57
  10.9 1.8 gather_fusion.1
  12.7 0.2 broadcast_select_fusion
  12.9 30.6 %all_to_all.24 = bf16[4,64,4096]{2,1,0:T(8,128)(2,1)} all-to-all(bf16[4,64,4096]{2,1,0:T(8,128)(2,1)S(1)} %broadcast_select_fusion), channel_id=1, replica_groups=mesh['clus'=4,'split'=32] {'clus'}, dimensions={0} | all-to-all | bytes 4194304 | tf_op jit(solution)/shard_map/all_to_all | solution.py:43
  43.5 0.0 copy-start
  43.6 0.0 copy-start.2
  43.6 0.0 all-gather.3.cloned.1.call-update
  43.6 0.6 copy-done
  44.2 1.9 gather_fusion
  46.1 0.7 select_n.52
  46.8 3.2 %all-to-all-start = ((s32[4,64,1]{1,2,0:T(1,128)}), s32[4,64,1]{1,2,0:T(1,128)S(1)}, u32[]{:S(2)}, u32[]{:S(2)}) async-start(s32[4,64,1]{1,2,0:T(1,128)} %bitcast.2), calls=%async_computation | async-start | bytes 4096 | tf_op jit(solution)/shard_map/all_to_all | solution.py:44
  50.0 5.1 %all-to-all-done = s32[4,64,1]{1,2,0:T(1,128)S(1)} async-done(((s32[4,64,1]{1,2,0:T(1,128)}), s32[4,64,1]{1,2,0:T(1,128)S(1)}, u32[]{:S(2)}, u32[]{:S(2)}) %all-to-all-start) | async-done | bytes 1056 | tf_op jit(solution)/shard_map/all_to_all | solution.py:44
  55.1 0.5 broadcast.98
  55.6 0.7 reduce.8
  56.2 0.1 eq.49
  56.3 0.1 reshape.103
  56.4 25.7 %all-gather = s32[32,1,256]{2,1,0:T(1,128)S(1)} all-gather(s32[1,1,256]{2,1,0:T(1,128)S(1)} %reshape.103), channel_id=1, replica_groups=mesh['clus'=4,'split'=32] {'split'}, dimensions={0}, use_global_device_ids=true | all-gather | bytes 33792 | tf_op jit(solution)/shard_map/all_gather | solution.py:52
  82.1 163.5 %all-gather.3.cloned.1.call-done = bf16[8192,4096]{1,0:T(8,128)(2,1)} async-done(((bf16[256,4096]{1,0:T(8,128)(2,1)}), bf16[8192,4096]{1,0:T(8,128)(2,1)}) %all-gather.3.cloned.1.call-update) | async-done | bytes 67108880 | tf_op jit(solution)/shard_map/all_gather | solution.py:51
  245.6 0.0 copy-done.2
  245.6 29.4 %fusion.1 = f32[256]{0:T(256)S(1)} fusion(bf16[256,4096]{1,0:T(8,128)(2,1)S(1)} %bitcast.14, bf16[8192,4096]{1,0:T(8,128)(2,1)} %all-gather.3.cloned.1.call-done, s32[256]{0:T(256)S(1)} %iota_add_fusion, pred[256]{0:T(512)(128)(4,1)S(1)} %broadcast_compare_fusion, s32[8192]{0:T(1024)S(1)} %bitcast.15, s32[256]{0:T(256)S(1)} %eq.49), kind=kOutput, calls=%fused_computation.9 | convolution fusion | flops 17192452096 | bytes 69242112 | tf_op jit(solution)/shard_map/dot_general | solution.py:8
  275.0 0.7 max_broadcast_in_dim.14
  275.6 4.2 %all-to-all-start.2 = ((f32[4,64,1]{1,2,0:T(1,128)}), f32[4,64,1]{1,2,0:T(1,128)S(1)}, u32[]{:S(2)}, u32[]{:S(2)}) async-start(f32[4,64,1]{1,2,0:T(1,128)} %bitcast.6), calls=%async_computation.2 | async-start | bytes 4096 | tf_op jit(solution)/shard_map/all_to_all | solution.py:56
  279.9 5.1 %all-to-all-done.2 = f32[4,64,1]{1,2,0:T(1,128)S(1)} async-done(((f32[4,64,1]{1,2,0:T(1,128)}), f32[4,64,1]{1,2,0:T(1,128)S(1)}, u32[]{:S(2)}, u32[]{:S(2)}) %all-to-all-start.2) | async-done | bytes 1056 | tf_op jit(solution)/shard_map/all_to_all | solution.py:56
  285.0 0.5 broadcast.99
  285.5 0.7 reduce.9
  286.2 0.1 all_to_all.20
  286.3 1.8 gather_fusion.2
  (8 shorter events, 0.0 us)
Async XLA Ops:
  6.5 4.0 %copy-start.1 = (f32[128,4096]{1,0:T(8,128)S(1)}, f32[128,4096]{1,0:T(8,128)}, u32[]{:S(2)}) copy-start(f32[128,4096]{1,0:T(8,128)} %param.2) | copy-start | bytes 6291460
  6.5 239.0 %all-gather.3.cloned.1.call-start = ((), (), s32[]{:S(2)}) async-start(), calls=%async_computation.3 | async-start | bytes 69206016 | tf_op jit(solution)/shard_map/all_gather | solution.py:51
  43.5 0.7 copy-start
  43.6 202.0 %copy-start.2 = (bf16[4,64,4096]{2,1,0:T(8,128)(2,1)S(1)}, bf16[4,64,4096]{2,1,0:T(8,128)(2,1)}, u32[]{:S(2)}) copy-start(bf16[4,64,4096]{2,1,0:T(8,128)(2,1)} %all_to_all.24) | copy-start | bytes 6291460
  46.8 8.3 %all-to-all-start = ((s32[4,64,1]{1,2,0:T(1,128)}), s32[4,64,1]{1,2,0:T(1,128)S(1)}, u32[]{:S(2)}, u32[]{:S(2)}) async-start(s32[4,64,1]{1,2,0:T(1,128)} %bitcast.2), calls=%async_computation | async-start | bytes 4096 | tf_op jit(solution)/shard_map/all_to_all | solution.py:44
  275.6 9.4 %all-to-all-start.2 = ((f32[4,64,1]{1,2,0:T(1,128)}), f32[4,64,1]{1,2,0:T(1,128)S(1)}, u32[]{:S(2)}, u32[]{:S(2)}) async-start(f32[4,64,1]{1,2,0:T(1,128)} %bitcast.6), calls=%async_computation.2 | async-start | bytes 4096 | tf_op jit(solution)/shard_map/all_to_all | solution.py:56
Sparse Core Ops, SparseCore 0:
  43.7 201.8 all-gather.2
where the time goes:
time: 295 us
  waiting for transfers between devices  174 us (59%)
  blocking collectives  56.3 us (19%)
  matrix products  29.4 us (10%)
  between operations  13.5 us (5%)
  local copies, waits for them, and re-layouts  8.82 us (3%)
  starting transfers between devices  7.47 us (3%)
  other arithmetic  5.76 us (2%)
    all_gather x1, waiting for transfers between devices, on_device(): lax.all_gather(unit, 'split', axis=0, tiled=True)  164 us
    all_to_all x1, blocking collectives, on_device(): lax.all_to_all(outgoing_unit, 'clus', split_axis=0, concat_axis=0, tiled=...  30.6 us
    dot_general x1, matrix products, masked_scores(): lax.dot_general(left, right, (((1,), (1,)), ((), ())), preferred_element_...  29.4 us
    all_gather x1, blocking collectives, on_device(): lax.all_gather(labels, 'split', axis=0, tiled=True)  25.7 us
  transfers between devices with their start and end apart: 3, of which 3 were waited for; matrix products, arithmetic and copies ran while one was open for 1% of the time, Pallas kernels for 0%

commit v1 on v0

--- a/solution.py
+++ b/solution.py
@@ -2,6 +2,7 @@
 import jax.numpy as jnp
 from jax import lax
 from jax.sharding import PartitionSpec as P
+from jax.lax import all_to_all, axis_size
 
 
 def masked_scores(left, left_ids, right, right_ids, left_start):
@@ -45,10 +46,16 @@
     )
     own_start = lax.axis_index("split") * slots
     floor_values = jnp.full((slots,), -1.0, jnp.float32)
+    strings_expand = lambda u: jnp.concatenate(
+        all_to_all(
+            jnp.stack(axis_size("split") * [u]), axis_name="split", concat_axis=0, split_axis=0
+        ),
+        axis=0,
+    )
     scores = masked_scores(
         unit,
         labels,
-        lax.all_gather(unit, "split", axis=0, tiled=True),
+        strings_expand(unit),
         lax.all_gather(labels, "split", axis=0, tiled=True),
         own_start,
     )

time: 295 us -> 990 us (3.36)
  blocking collectives: 56.3 us -> 901 us
  waiting for transfers between devices: 174 us -> 5.06 us
  local copies, waits for them, and re-layouts: 8.82 us -> 29.3 us
  between operations: 13.5 us -> 0.1 us
    all_gather x1, blocking collectives: 25.7 us -> 870 us  [on_device(): lax.all_gather(labels, 'split', axis=0, tiled=True)]
    all_gather x1 -> x0, waiting for transfers between devices: 164 us -> none  [on_device(): lax.all_gather(unit, 'split', axis=0, tiled=True)]
    another operation x0 -> x1, local copies, waits for them, and re-layouts: none -> 21 us  [on_device(): jnp.stack(axis_size('split') * [u])]
  transfers between devices with their start and end apart: 3 -> 3, of which waited for: 3 -> 1; matrix products, arithmetic and copies ran while one was open for 1% -> 1% of each run, Pallas kernels for 0% -> 0%
where the time goes in v1:
time: 990 us; the launch traced here: 988 us
  blocking collectives  901 us (91%)
  local copies, waits for them, and re-layouts  29.3 us (3%)
  matrix products  29.3 us (3%)
  starting transfers between devices  16.1 us (2%)
    all_gather x1, blocking collectives, on_device(): lax.all_gather(labels, 'split', axis=0, tiled=True)  870 us
    all_to_all x1, blocking collectives, on_device(): lax.all_to_all(outgoing_unit, 'clus', split_axis=0, concat_axis=0, tiled=...  30.6 us
    dot_general x1, matrix products, masked_scores(): lax.dot_general(left, right, (((1,), (1,)), ((), ())), preferred_element_...  29.3 us
    another operation x1, local copies, waits for them, and re-layouts, on_device(): jnp.stack(axis_size('split') * [u])  21 us
  transfers between devices with their start and end apart: 3, of which 1 were waited for; matrix products, arithmetic and copies ran while one was open for 1% of the time, Pallas kernels for 0%

profile of v1, /device:TPU:0, one launch (start us, length us, event | category | flops | bytes accessed | tf_op | source)
XLA Modules:
  0.0 987.7 jit_solution(2911523991870402585)
XLA Ops:
  0.0 0.0 copy-start
  0.0 0.8 and_select_fusion
  0.8 0.1 fusion.3
  0.9 0.2 reduce_window_sum.11
  1.1 0.2 select_reduce_fusion.1
  1.3 0.7 compare_select_fusion.1
  1.9 0.1 select_reduce_fusion
  2.0 0.1 fusion.2
  2.2 1.9 gather_fusion
  4.1 0.7 select_n.52
  4.8 4.4 all-to-all-start
  9.2 0.1 broadcast_in_dim.57
  9.2 1.8 multiply_reduce_fusion
  11.1 0.0 copy-done
  11.1 0.2 multiply_convert_fusion
  11.3 1.8 gather_fusion.1
  13.2 1.6 broadcast_select_fusion
  14.7 0.0 all-to-all-done
  14.7 30.6 %all_to_all.29 = bf16[4,64,4096]{2,1,0:T(8,128)(2,1)S(1)} all-to-all(bf16[4,64,4096]{2,1,0:T(8,128)(2,1)} %broadcast_select_fusion), channel_id=1, replica_groups=mesh['clus'=4,'split'=32] {'clus'}, dimensions={0} | all-to-all | bytes 4194304 | tf_op jit(solution)/shard_map/all_to_all | solution.py:44
  45.3 21.0 %stack.2 = bf16[32,256,4096]{2,1,0:T(8,128)(2,1)} broadcast(bf16[256,4096]{1,0:T(8,128)(2,1)S(1)} %bitcast.13), dimensions={1,2} | broadcast | bytes 69206016 | tf_op jit(solution)/shard_map/stack | solution.py:51
  66.3 8.5 all-to-all-start.2
  74.8 0.5 broadcast.99
  75.3 0.7 reduce.8
  76.0 0.1 eq.49
  76.1 0.1 reshape.110
  76.2 870.2 %all-gather = s32[32,1,256]{2,1,0:T(1,128)S(1)} all-gather(s32[1,1,256]{2,1,0:T(1,128)S(1)} %reshape.110), channel_id=1, replica_groups=mesh['clus'=4,'split'=32] {'split'}, dimensions={0}, use_global_device_ids=true | all-gather | bytes 33792 | tf_op jit(solution)/shard_map/all_gather | solution.py:59
  946.3 0.0 all-to-all-done.2
  946.3 29.3 %fusion.1 = f32[256]{0:T(256)S(1)} fusion(bf16[256,4096]{1,0:T(8,128)(2,1)S(1)} %bitcast.14, bf16[8192,4096]{1,0:T(8,128)(2,1)} %bitcast.6, s32[256]{0:T(256)S(1)} %iota_add_fusion, pred[256]{0:T(512)(128)(4,1)S(1)} %broadcast_compare_fusion, s32[8192]{0:T(1024)S(1)} %bitcast.16, s32[256]{0:T(256)S(1)} %eq.49), kind=kOutput, calls=%fused_computation.9 | convolution fusion | flops 17192452096 | bytes 69242112 | tf_op jit(solution)/shard_map/dot_general | solution.py:9
  975.7 0.7 max_broadcast_in_dim.14
  976.3 3.2 all-to-all-start.3
  979.6 5.1 all-to-all-done.3
  984.7 0.5 broadcast.100
  985.2 0.7 reduce.9
  985.8 0.1 all_to_all.24
  985.9 1.8 gather_fusion.2
  (8 shorter events, 0.0 us)
Async XLA Ops:
  0.0 11.1 %copy-start = (f32[128,4096]{1,0:T(8,128)S(1)}, f32[128,4096]{1,0:T(8,128)}, u32[]{:S(2)}) copy-start(f32[128,4096]{1,0:T(8,128)} %param.2) | copy-start | bytes 6291460
  4.8 9.9 %all-to-all-start = ((s32[4,64,1]{1,2,0:T(1,128)}), s32[4,64,1]{1,2,0:T(1,128)S(1)}, u32[]{:S(2)}, u32[]{:S(2)}) async-start(s32[4,64,1]{1,2,0:T(1,128)} %bitcast.2), calls=%async_computation | async-start | bytes 4096 | tf_op jit(solution)/shard_map/all_to_all | solution.py:45
  66.3 880.0 %all-to-all-start.2 = ((bf16[32,256,4096]{2,1,0:T(8,128)(2,1)}), bf16[32,256,4096]{2,1,0:T(8,128)(2,1)}, u32[]{:S(2)}, u32[]{:S(2)}) async-start(bf16[32,256,4096]{2,1,0:T(8,128)(2,1)} %stack.2), calls=%async_computation.2 | async-start | bytes 134217728 | tf_op jit(solution)/shard_map/all_to_all | solution.py:50
  976.3 8.3 all-to-all-start.3
